TPU v7x, 512 devices: a whole 4x4x16 slice. The times are simulated.
512 devices in a mesh: ctx: 64 (over y, z), ch: 8 (over x, core).
Axes of the slice: x: 4, y: 4, z: 16, core: 2. Of those that a mesh axis runs over, the one named last changes fastest.
Arguments:
- query_rows: bfloat16 [8192, 8192], P('ctx', 'ch'), may hold values from -6 to 6
- key_rows: bfloat16 [8192, 8192], P('ctx', 'ch'), may hold values from -6 to 6
- value_rows: bfloat16 [8192, 8192], P('ctx', 'ch'), may hold values from -6 to 6
- short_filter: float32 [3, 3, 8192], P(None, None, 'ch'), may hold values from -3.5 to 3.5
- decay_rate: float32 [8192, 16], P('ch'), may hold values from 2e-05 to 0.1
- residues: float32 [8192, 16], P('ch'), may hold values from -1.5 to 1.5
- out_weight: bfloat16 [8192, 4096], P('ctx', 'ch'), may hold values from -0.1875 to 0.1875
- record_starts: int32 [4], replicated, may hold values from 0 to 8191, as said below
Outputs:
- block_out: bfloat16 [8192, 4096], P('ctx', 'ch')
Inputs may be any that keep to these rules, and one draw needn't show every extreme that they name: record_starts[0] is 0 and the last entry is 8191; the entries are distinct and increasing, and all but the first lie in the second half of the 8192 tokens.
All inputs are finite; a program needn't handle non-finite values.
Results may differ from a plain program's by a relative error of at most 0.017.
Values may be sent and summed in bfloat16 or wider, within the bound.
A program may use at most 64 MiB of HBM per device.

v0:
```python
import jax
import jax.numpy as jnp
from jax import lax
from jax.sharding import PartitionSpec as P

MODES = 16
KS = 3


def shifted(block, axis, distance):
    devices = range(lax.axis_size(axis))
    route = [(i - distance, i) for i in devices if i - distance in devices]
    return lax.ppermute(block, axis, route)


def carried_in(x, axis, combine, identity):
    devices, mine = (lax.axis_size(axis), lax.axis_index(axis))
    everything = jax.tree.map(lambda part: lax.all_gather(part, axis), x)
    start = jax.tree.map(
        lambda part, zero: jnp.broadcast_to(jnp.asarray(zero, part.dtype), part.shape), x, identity
    )

    def hop(k, before):
        reached = k < mine
        new = combine(before, jax.tree.map(lambda part: part[k], everything))
        return jax.tree.map(lambda a, b: jnp.where(reached, a, b), new, before)

    return lax.fori_loop(0, devices, hop, start)


def ages_of(positions, record_starts):
    earlier = record_starts[None, :] <= positions[:, None]
    segment = jnp.max(jnp.where(earlier, record_starts[None, :], 0), axis=1)
    return positions - segment


def masked_conv(extended, weights, ages, count):
    taps = weights.shape[0]
    total = jnp.zeros((count, extended.shape[1]), jnp.float32)
    for tap_index in range(taps):
        keeper = (ages >= tap_index).astype(jnp.float32)[:, None]
        window = extended[taps - 1 - tap_index : taps - 1 - tap_index + count]
        total = total + weights[tap_index][None, :] * window * keeper
    return total


def combine_pairs(earlier, later_pair):
    return (earlier[0] * later_pair[0], later_pair[0] * earlier[1] + later_pair[1])


def local(
    query_rows, key_rows, value_rows, short_filter, decay_rate, residues, out_weight, record_starts
):
    row_count, channels = query_rows.shape
    anchor = lax.axis_index("ctx") * row_count
    positions = anchor + jnp.arange(row_count, dtype=jnp.int32)
    ages = ages_of(positions, record_starts)
    reach_short = KS - 1
    tails = shifted(
        (
            query_rows[row_count - reach_short :],
            key_rows[row_count - reach_short :],
            value_rows[row_count - reach_short :],
        ),
        "ctx",
        1,
    )
    query_conv = masked_conv(
        jnp.concatenate([tails[0], query_rows], axis=0).astype(jnp.float32),
        short_filter[0],
        ages,
        row_count,
    )
    key_conv = masked_conv(
        jnp.concatenate([tails[1], key_rows], axis=0).astype(jnp.float32),
        short_filter[1],
        ages,
        row_count,
    )
    value_conv = masked_conv(
        jnp.concatenate([tails[2], value_rows], axis=0).astype(jnp.float32),
        short_filter[2],
        ages,
        row_count,
    )
    mixed = (key_conv * value_conv).astype(jnp.bfloat16).astype(jnp.float32)
    gain = jnp.sqrt(1.0 - jnp.exp(-2.0 * decay_rate))
    block_rows = 8
    block_count = row_count // block_rows
    inner_index = jnp.arange(block_rows, dtype=jnp.float32)
    inner_ints = jnp.arange(block_rows, dtype=jnp.int32)
    rising = jnp.exp(-decay_rate[None, :, :] * inner_index[:, None, None])
    taps_inner = jnp.sum(rising * (residues * gain)[None, :, :], axis=2)
    local_index = jnp.arange(row_count, dtype=jnp.int32)
    inner_ages = jnp.minimum(ages, local_index % block_rows)
    padded_mixed = jnp.concatenate(
        [jnp.zeros((block_rows - 1, channels), jnp.float32), mixed], axis=0
    )
    within = masked_conv(padded_mixed, taps_inner, inner_ages, row_count)
    entry_powers = jnp.exp(-decay_rate[None, :, :] * (inner_index[:, None, None] + 1.0))
    final_powers = (
        jnp.exp(-decay_rate[None, :, :] * (block_rows - 1.0 - inner_index[:, None, None]))
        * gain[None, :, :]
    )
    block_decay = jnp.exp(-decay_rate * block_rows)
    mixed_blocks = mixed.reshape(block_count, block_rows, channels)
    age_blocks = ages.reshape(block_count, block_rows)
    last_ages = age_blocks[:, block_rows - 1]
    weighted = (last_ages[:, None] >= block_rows - 1 - inner_ints[None, :]).astype(jnp.float32)
    endings = jnp.einsum("rcm,brc->bcm", final_powers, mixed_blocks * weighted[:, :, None])
    unbroken = (last_ages >= block_rows).astype(jnp.float32)

    def advance(state, inputs):
        ending, kept = inputs
        return (block_decay * kept * state + ending, state)

    local_state, entering_states = lax.scan(
        advance, jnp.zeros((channels, MODES), jnp.float32), (endings, unbroken)
    )
    entering = (age_blocks > inner_ints[None, :]).astype(jnp.float32)
    between = (
        jnp.einsum("rcm,bcm->brc", entry_powers, residues[None, :, :] * entering_states)
        * entering[:, :, None]
    )
    device_decay = jnp.exp(-decay_rate * row_count) * (ages[row_count - 1] >= row_count).astype(
        jnp.float32
    )
    identity_pair = (jnp.ones_like(device_decay), jnp.zeros_like(local_state))
    carried = carried_in((device_decay, local_state), "ctx", combine_pairs, identity_pair)[1]
    block_index = jnp.arange(block_count, dtype=jnp.float32)
    block_starts = jnp.exp(-decay_rate[None, :, :] * (block_index[:, None, None] * block_rows))
    coefficient = block_starts * (residues * carried)[None, :, :]
    correction = jnp.einsum("rcm,bcm->brc", entry_powers, coefficient).reshape(row_count, channels)
    untouched = (ages > local_index).astype(jnp.float32)[:, None]
    filtered = within + between.reshape(row_count, channels) + correction * untouched
    gated = (query_conv * filtered).astype(jnp.bfloat16)
    all_channels = lax.all_gather(gated, "ch", axis=1, tiled=True)
    result = jnp.dot(
        all_channels,
        lax.all_gather(out_weight, "ctx", axis=0, tiled=True),
        preferred_element_type=jnp.float32,
    )
    return result.astype(jnp.bfloat16)


def solution(mesh):
    return jax.shard_map(
        local,
        mesh=mesh,
        in_specs=(
            P("ctx", "ch"),
            P("ctx", "ch"),
            P("ctx", "ch"),
            P(None, None, "ch"),
            P("ch", None),
            P("ch", None),
            P("ctx", "ch"),
            P(),
        ),
        out_specs=P("ctx", "ch"),
        check_vma=False,
    )
```

profile of v0, /device:TPU:32, one launch (start us, length us, event | category | flops | bytes accessed | tf_op | source)
XLA Modules:
  0.0 616.6 jit_solution(5873278730106274515)
XLA Ops:
  7.3 3.8 collective-permute-start.1
  11.8 3.8 collective-permute-start.2
  17.6 1.6 fusion.59
  23.6 2.8 copy.59
  26.3 5.7 fusion.16
  32.1 5.2 copy.61
  37.3 32.3 %while.27 = (s32[]{:T(128)}, f32[1024,16]{0,1:T(8,128)S(1)}, f32[16,1024,16]{1,2,0:T(8,128)}, f32[16]{0:T(128)S(1)}, f32[1024,16]{0,1:T(8,128)S(1)}, /*index=5*/f32[16,1024,16]{1,2,0:T(8,128)S(1)}, s32[]{:T(128)}, s32[]{:T(128)}) while((s32[]{:T(128)}, f32[1024,16]{0,1:T(8,128)S(1)}, f32[16,1024,16]{1,2,0:T(8,128)}, ...), condition=%wide.region_3.4_spmd.clone, body=%wide.region_2.3_spmd.clone.sunk | while | flops 81923 | bytes 393844 | solution.py:117
  70.3 5.0 collective-permute-start
  76.8 2.1 slice_reduce_fusion.7
  79.1 4.9 copy.62
  84.0 6.5 %multiply_bitcast_fusion = f32[16,8,1024]{0,1,2:T(8,128)} fusion(bf16[16,1024,16]{2,0,1:T(8,128)(2,1)} %copy.62, f32[16,8]{0,1:T(8,128)S(1)} %copy.63, f32[8]{0:T(128)S(1)} %iota_add_fusion, f32[1024,16]{1,0:T(8,128)S(1)} %copy.57), kind=kOutput, calls=%fused_computation.16 | convolution fusion | flops 4456448 | bytes 1114656 | tf_op jit(solution)/shard_map/rcm,bcm->brc/dot_general | solution.py:122
  90.5 3.0 copy.64
  93.6 74.4 %all-gather.11.cloned.1.call-done = f32[65536,16]{0,1:T(8,128)} async-done(((f32[1024,16]{0,1:T(8,128)}), f32[65536,16]{0,1:T(8,128)}) %all-gather.11.cloned.1.call-update) | async-done | bytes 4194320 | tf_op jit(solution)/shard_map/all_gather | solution.py:18
  168.0 6.5 %copy.72 = f32[2,8,64,1024]{3,2,1,0:T(8,128)} copy(f32[2,8,64,1024]{3,1,2,0:T(8,128)} %bitcast.68) | data formatting | bytes 8388608
  174.5 137.7 %all-gather.13.cloned.1.call-done = f32[65536,16]{0,1:T(8,128)} async-done(((f32[1024,16]{0,1:T(8,128)}), f32[65536,16]{0,1:T(8,128)}) %all-gather.13.cloned.1.call-update) | async-done | bytes 4194320 | tf_op jit(solution)/shard_map/all_gather | solution.py:18
  312.3 6.6 %copy.73 = f32[2,8,64,1024]{3,2,1,0:T(8,128)} copy(f32[2,8,64,1024]{3,1,2,0:T(8,128)} %bitcast.69) | data formatting | bytes 8388608
  318.9 88.1 %while.28 = (s32[]{:T(128)}, f32[1024,16]{0,1:T(8,128)S(1)}, s32[]{:T(128)}, f32[64,1024,16]{1,0,2:T(8,128)}, f32[64,1024,16]{1,0,2:T(8,128)}, /*index=5*/s32[]{:T(128)}, s32[]{:T(128)}) while((s32[]{:T(128)}, f32[1024,16]{0,1:T(8,128)S(1)}, s32[]{:T(128)}, f32[64,1024,16]{1,0,2:T(8,128)}, f32[64,1024,16]{1,0,2:T(8,128)}, ...), condition=%wide.region_5.6_spmd.clone, body=%wide.region_4.5_spmd.clone.sunk | while | flops 65540 | bytes 524389 | solution.py:28
  320.2 1.3 constant_dynamic-slice_fusion.3
  321.6 1.3 constant_dynamic-slice_fusion.3
  323.0 1.3 constant_dynamic-slice_fusion.3
  324.4 1.3 constant_dynamic-slice_fusion.3
  325.7 1.3 constant_dynamic-slice_fusion.3
  327.1 1.3 constant_dynamic-slice_fusion.3
  328.5 1.3 constant_dynamic-slice_fusion.3
  329.9 1.3 constant_dynamic-slice_fusion.3
  331.2 1.3 constant_dynamic-slice_fusion.3
  332.6 1.3 constant_dynamic-slice_fusion.3
  334.0 1.3 constant_dynamic-slice_fusion.3
  335.4 1.3 constant_dynamic-slice_fusion.3
  338.1 1.3 constant_dynamic-slice_fusion.3
  339.5 1.3 constant_dynamic-slice_fusion.3
  340.9 1.3 constant_dynamic-slice_fusion.3
  342.3 1.3 constant_dynamic-slice_fusion.3
  345.0 1.3 constant_dynamic-slice_fusion.3
  346.4 1.3 constant_dynamic-slice_fusion.3
  347.8 1.3 constant_dynamic-slice_fusion.3
  349.1 1.3 constant_dynamic-slice_fusion.3
  350.5 1.3 constant_dynamic-slice_fusion.3
  351.9 1.3 constant_dynamic-slice_fusion.3
  353.3 1.3 constant_dynamic-slice_fusion.3
  354.6 1.3 constant_dynamic-slice_fusion.3
  356.0 1.3 constant_dynamic-slice_fusion.3
  407.2 3.9 fusion.21
  411.0 3.0 copy.69
  414.0 1.7 fusion.47
  416.3 27.3 %all-gather.7.cloned.1.call-done = bf16[128,8192]{1,0:T(8,128)(2,1)} async-done(((bf16[128,1024]{1,0:T(8,128)(2,1)}), bf16[128,8192]{1,0:T(8,128)(2,1)}) %all-gather.7.cloned.1.call-update) | async-done | bytes 2097168 | tf_op jit(solution)/shard_map/all_gather | solution.py:137
  443.7 160.5 %all-gather.9.cloned.1.call-done = bf16[8192,512]{1,0:T(8,128)(2,1)} async-done(((bf16[128,512]{1,0:T(8,128)(2,1)}), bf16[8192,512]{1,0:T(8,128)(2,1)}) %all-gather.9.cloned.1.call-update) | async-done | bytes 8388624 | tf_op jit(solution)/shard_map/all_gather | solution.py:140
  604.1 5.9 convolution_convert_fusion
  (203 shorter events, 95.7 us)
Async XLA Ops:
  6.5 161.5 %all-gather.11.cloned.1.call-start = ((), (), s32[]{:S(2)}) async-start(), calls=%async_computation.2 | async-start | bytes 4259840 | tf_op jit(solution)/shard_map/all_gather | solution.py:18
  7.3 13.7 %collective-permute-start.1 = (bf16[2,1024]{1,0:T(2,128)(2,1)S(1)}, bf16[2,1024]{1,0:T(2,128)(2,1)S(1)}, u32[]{:S(2)}, u32[]{:S(2)}) collective-permute-start(bf16[2,1024]{1,0:T(2,128)(2,1)S(1)} %slice.146), channel_id=1, source_target_pairs={{0,8},{8,16},{16,24},{24,32},{32,40},{40,48},{48,56},{56,64},{64,7... | collective-permute-start | bytes 12296 | tf_op jit(solution)/shard_map/ppermute | solution.py:13
  11.8 10.2 %collective-permute-start.2 = (bf16[2,1024]{1,0:T(2,128)(2,1)S(1)}, bf16[2,1024]{1,0:T(2,128)(2,1)S(1)}, u32[]{:S(2)}, u32[]{:S(2)}) collective-permute-start(bf16[2,1024]{1,0:T(2,128)(2,1)S(1)} %slice.153), channel_id=1, source_target_pairs={{0,8},{8,16},{16,24},{24,32},{32,40},{40,48},{48,56},{56,64},{64,7... | collective-permute-start | bytes 12296 | tf_op jit(solution)/shard_map/ppermute | solution.py:13
  19.2 293.1 %all-gather.13.cloned.1.call-start = ((), (), s32[]{:S(2)}) async-start(), calls=%async_computation.3 | async-start | bytes 4259840 | tf_op jit(solution)/shard_map/all_gather | solution.py:18
  32.1 38.2 %copy-start.3 = (bf16[128,1024]{1,0:T(8,128)(2,1)S(1)}, bf16[128,1024]{1,0:T(8,128)(2,1)}, u32[]{:S(2)}) copy-start(bf16[128,1024]{1,0:T(8,128)(2,1)} %param.12) | copy-start | bytes 786436
  37.3 41.7 %copy-start.2 = (f32[1024,16]{0,1:T(8,128)S(1)}, f32[1024,16]{0,1:T(8,128)}, u32[]{:S(2)}) copy-start(f32[1024,16]{0,1:T(8,128)} %param.17) | copy-start | bytes 196612
  69.6 0.6 copy-start
  69.6 9.4 %copy-start.1 = (f32[16,1024,16]{1,2,0:T(8,128)S(1)}, f32[16,1024,16]{1,2,0:T(8,128)}, u32[]{:S(2)}) copy-start(f32[16,1024,16]{1,2,0:T(8,128)} %get-tuple-element.132) | copy-start | bytes 3145732
  70.2 373.5 %all-gather.7.cloned.1.call-start = ((), (), s32[]{:S(2)}) async-start(), calls=%async_computation | async-start | bytes 2359296 | tf_op jit(solution)/shard_map/all_gather | solution.py:137
  70.3 23.2 %collective-permute-start = (bf16[2,1024]{1,0:T(2,128)(2,1)S(1)}, bf16[2,1024]{1,0:T(2,128)(2,1)S(1)}, u32[]{:S(2)}, u32[]{:S(2)}) collective-permute-start(bf16[2,1024]{1,0:T(2,128)(2,1)S(1)} %slice.138), channel_id=1, source_target_pairs={{0,8},{8,16},{16,24},{24,32},{32,40},{40,48},{48,56},{56,64},{64,7... | collective-permute-start | bytes 12296 | tf_op jit(solution)/shard_map/ppermute | solution.py:13
  415.8 188.4 %all-gather.9.cloned.1.call-start = ((), (), s32[]{:S(2)}) async-start(), calls=%async_computation.1 | async-start | bytes 8519680 | tf_op jit(solution)/shard_map/all_gather | solution.py:140
Sparse Core Ops, SparseCore 0:
  19.3 148.6 all-gather.10
  171.0 141.2 all-gather.12
  415.9 27.7 all-gather.6
  446.5 157.6 all-gather.8
where the time goes:
time: 619 us; the launch traced here: 617 us
  waiting for transfers between devices  401 us (65%)
  local copies, waits for them, and re-layouts  133 us (21%)
  other arithmetic  32.3 us (5%)
  matrix products  22.1 us (4%)
  between operations  14.1 us (2%)
  starting transfers between devices  12.8 us (2%)
    all_gather x2, waiting for transfers between devices, carried_in(): everything = jax.tree.map(lambda part: lax.all_gather(part, axis), x)  212 us
    all_gather x1, waiting for transfers between devices, local(): lax.all_gather(out_weight, 'ctx', axis=0, tiled=True)  160 us
    dynamic_slice x64, local copies, waits for them, and re-layouts, hop(): new = combine(before, jax.tree.map(lambda part: part[k], everything))  83.4 us
    all_gather x1, waiting for transfers between devices, local(): all_channels = lax.all_gather(gated, 'ch', axis=1, tiled=True)  27.3 us
    unnamed x11, local copies, waits for them, and re-layouts  18.9 us
    ppermute x3, starting transfers between devices, shifted(): return lax.ppermute(block, axis, route)  12.7 us
  transfers between devices with their start and end apart: 7, of which 4 were waited for; matrix products, arithmetic and copies ran while one was open for 13% of the time, Pallas kernels for 0%

commit v1 on v0

--- a/solution.py
+++ b/solution.py
@@ -134,7 +134,9 @@
     untouched = (ages > local_index).astype(jnp.float32)[:, None]
     filtered = within + between.reshape(row_count, channels) + correction * untouched
     gated = (query_conv * filtered).astype(jnp.bfloat16)
-    all_channels = lax.all_gather(gated, "ch", axis=1, tiled=True)
+    all_channels = jnp.concatenate(
+        lax.all_to_all(jnp.stack([gated] * lax.psum(1, "ch")), "ch", 0, 0), axis=1
+    )
     result = jnp.dot(
         all_channels,
         lax.all_gather(out_weight, "ctx", axis=0, tiled=True),

time: 619 us -> 482 us (0.78)
  the two profiles are of different devices: /device:TPU:32 before, /device:TPU:2 now
where the time goes in v1:
time: 482 us; the launch traced here: 479 us
  waiting for transfers between devices  236 us (49%)
  local copies, waits for them, and re-layouts  133 us (28%)
  other arithmetic  30.7 us (6%)
  blocking collectives  30.7 us (6%)
  matrix products  21.5 us (4%)
  between operations  14.1 us (3%)
  starting transfers between devices  11.5 us (2%)
    all_gather x2, waiting for transfers between devices, carried_in(): everything = jax.tree.map(lambda part: lax.all_gather(part, axis), x)  216 us
    dynamic_slice x64, local copies, waits for them, and re-layouts, hop(): new = combine(before, jax.tree.map(lambda part: part[k], everything))  83.6 us
    all_to_all x1, blocking collectives, local(): lax.all_to_all(jnp.stack([gated] * lax.psum(1, 'ch')), 'ch', 0, 0)  30.7 us
    all_gather x1, waiting for transfers between devices, local(): lax.all_gather(out_weight, 'ctx', axis=0, tiled=True)  20 us
    unnamed x11, local copies, waits for them, and re-layouts  19 us
    ppermute x3, starting transfers between devices, shifted(): return lax.ppermute(block, axis, route)  11.4 us
    add x16, other arithmetic, advance(): return (block_decay * kept * state + ending, state)  10.4 us
    dynamic_update_slice x16, other arithmetic, local(): lax.scan(advance, jnp.zeros((channels, MODES), jnp.float32), (endings, un...  10 us
  transfers between devices with their start and end apart: 6, of which 3 were waited for; matrix products, arithmetic and copies ran while one was open for 37% of the time, Pallas kernels for 0%

profile of v1, /device:TPU:2, one launch (start us, length us, event | category | flops | bytes accessed | tf_op | source)
XLA Modules:
  0.0 479.3 jit_solution(13294364404282448633)
XLA Ops:
  7.3 3.8 collective-permute-start.1
  11.8 3.8 collective-permute-start.2
  17.6 1.6 fusion.59
  23.6 2.8 copy.62
  26.3 5.7 %fusion.16 = f32[16,1024,16]{2,0,1:T(8,128)} fusion(f32[16,8,1024]{0,1,2:T(8,128)} %copy.62, f32[1024,16]{1,0:T(8,128)S(1)} %copy.63, f32[8]{0:T(128)S(1)} %iota_subtract_fusion, f32[16,8]{0,1:T(8,128)S(1)} %compare_convert_fusion, f32[1024,16]{1,0:T(8,128)S(1)} %copy.60), kind=kOutput, calls=%fused_computation.25 | convolution fusion | flops 4587520 | bytes 1704480 | tf_op jit(solution)/shard_map/rcm,brc->bcm/dot_general | solution.py:110
  32.1 5.2 %copy.64 = f32[16,1024,16]{1,2,0:T(8,128)S(1)} copy(f32[16,1024,16]{2,0,1:T(8,128)} %fusion.16) | data formatting | bytes 2097152
  37.3 30.5 %while.27 = (s32[]{:T(128)}, f32[1024,16]{0,1:T(8,128)S(1)}, f32[16,1024,16]{1,2,0:T(8,128)}, f32[16]{0:T(128)S(1)}, f32[1024,16]{0,1:T(8,128)S(1)}, /*index=5*/f32[16,1024,16]{1,2,0:T(8,128)S(1)}, s32[]{:T(128)}, s32[]{:T(128)}) while((s32[]{:T(128)}, f32[1024,16]{0,1:T(8,128)S(1)}, f32[16,1024,16]{1,2,0:T(8,128)}, ...), condition=%wide.region_3.4_spmd.clone, body=%wide.region_2.3_spmd.clone.sunk | while | flops 81923 | bytes 393844 | solution.py:117
  68.5 3.8 collective-permute-start
  73.9 2.1 slice_reduce_fusion.7
  76.2 4.9 %copy.65 = bf16[16,1024,16]{2,0,1:T(8,128)(2,1)} copy(bf16[16,1024,16]{1,2,0:T(8,128)(2,1)S(1)} %broadcast_multiply_fusion) | data formatting | bytes 1048576 | tf_op jit(solution)/shard_map/mul | solution.py:122
  81.1 6.5 %multiply_bitcast_fusion = f32[16,8,1024]{0,1,2:T(8,128)} fusion(bf16[16,1024,16]{2,0,1:T(8,128)(2,1)} %copy.65, f32[16,8]{0,1:T(8,128)S(1)} %copy.66, f32[8]{0:T(128)S(1)} %iota_add_fusion, f32[1024,16]{1,0:T(8,128)S(1)} %copy.60), kind=kOutput, calls=%fused_computation.16 | convolution fusion | flops 4456448 | bytes 1114656 | tf_op jit(solution)/shard_map/rcm,bcm->brc/dot_general | solution.py:122
  87.6 3.0 copy.67
  90.7 78.0 %all-gather.8.cloned.1.call-done = f32[65536,16]{0,1:T(8,128)} async-done(((f32[1024,16]{0,1:T(8,128)}), f32[65536,16]{0,1:T(8,128)}) %all-gather.8.cloned.1.call-update) | async-done | bytes 4194320 | tf_op jit(solution)/shard_map/all_gather | solution.py:18
  168.6 6.6 %copy.76 = f32[2,8,64,1024]{3,2,1,0:T(8,128)} copy(f32[2,8,64,1024]{3,1,2,0:T(8,128)} %bitcast.72) | data formatting | bytes 8388608
  175.2 137.7 %all-gather.10.cloned.1.call-done = f32[65536,16]{0,1:T(8,128)} async-done(((f32[1024,16]{0,1:T(8,128)}), f32[65536,16]{0,1:T(8,128)}) %all-gather.10.cloned.1.call-update) | async-done | bytes 4194320 | tf_op jit(solution)/shard_map/all_gather | solution.py:18
  312.9 6.6 %copy.77 = f32[2,8,64,1024]{3,2,1,0:T(8,128)} copy(f32[2,8,64,1024]{3,1,2,0:T(8,128)} %bitcast.73) | data formatting | bytes 8388608
  319.5 88.3 %while.28 = (s32[]{:T(128)}, f32[1024,16]{0,1:T(8,128)S(1)}, s32[]{:T(128)}, f32[64,1024,16]{1,0,2:T(8,128)}, f32[64,1024,16]{1,0,2:T(8,128)}, /*index=5*/s32[]{:T(128)}, s32[]{:T(128)}) while((s32[]{:T(128)}, f32[1024,16]{0,1:T(8,128)S(1)}, s32[]{:T(128)}, f32[64,1024,16]{1,0,2:T(8,128)}, f32[64,1024,16]{1,0,2:T(8,128)}, ...), condition=%wide.region_5.6_spmd.clone, body=%wide.region_4.5_spmd.clone.sunk | while | flops 65540 | bytes 524389 | solution.py:28
  320.9 1.3 constant_dynamic-slice_fusion.3
  322.3 1.3 constant_dynamic-slice_fusion.3
  323.6 1.3 constant_dynamic-slice_fusion.3
  325.0 1.3 constant_dynamic-slice_fusion.3
  326.4 1.3 constant_dynamic-slice_fusion.3
  329.1 1.3 constant_dynamic-slice_fusion.3
  330.5 1.3 constant_dynamic-slice_fusion.3
  331.9 1.3 constant_dynamic-slice_fusion.3
  333.3 1.3 constant_dynamic-slice_fusion.3
  337.4 1.3 constant_dynamic-slice_fusion.3
  341.5 1.3 constant_dynamic-slice_fusion.3
  347.0 1.3 constant_dynamic-slice_fusion.3
  348.4 1.3 constant_dynamic-slice_fusion.3
  352.6 1.3 constant_dynamic-slice_fusion.3
  355.3 1.3 constant_dynamic-slice_fusion.3
  359.5 1.3 constant_dynamic-slice_fusion.3
  367.7 1.3 constant_dynamic-slice_fusion.3
  369.1 1.3 constant_dynamic-slice_fusion.3
  370.5 1.3 constant_dynamic-slice_fusion.3
  371.9 1.3 constant_dynamic-slice_fusion.3
  373.3 1.3 constant_dynamic-slice_fusion.3
  377.4 1.3 constant_dynamic-slice_fusion.3
  396.7 1.4 constant_dynamic-slice_fusion.3
  402.3 1.3 constant_dynamic-slice_fusion.3
  403.6 1.3 constant_dynamic-slice_fusion.3
  406.4 1.3 constant_dynamic-slice_fusion.3
  408.1 3.9 fusion.21
  411.9 3.3 copy.72
  416.7 30.7 %all_to_all.5 = bf16[8,128,1024]{1,2,0:T(8,128)(2,1)S(1)} all-to-all(bf16[8,128,1024]{1,2,0:T(8,128)(2,1)S(1)} %stack.2), channel_id=1, replica_groups=mesh['ctx'=64,'ch'=8] {'ch'}, dimensions={0} | all-to-all | bytes 4194304 | tf_op jit(solution)/shard_map/all_to_all | solution.py:138
  447.4 20.0 %all-gather.6.cloned.1.call-done = bf16[8192,512]{1,0:T(8,128)(2,1)} async-done(((bf16[128,512]{1,0:T(8,128)(2,1)}), bf16[8192,512]{1,0:T(8,128)(2,1)}) %all-gather.6.cloned.1.call-update) | async-done | bytes 8388624 | tf_op jit(solution)/shard_map/all_gather | solution.py:142
  467.4 5.3 %convolution_convert_fusion = bf16[128,512]{1,0:T(8,128)(2,1)} fusion(bf16[128,8192]{0,1:T(8,128)(2,1)S(1)} %bitcast.68, bf16[8192,512]{1,0:T(8,128)(2,1)} %all-gather.6.cloned.1.call-done), kind=kOutput, calls=%fused_computation.35 | convolution fusion | flops 1073807360 | bytes 10616832 | tf_op jit(solution)/shard_map/dot_general | solution.py:140
  (203 shorter events, 93.7 us)
Async XLA Ops:
  6.5 162.1 %all-gather.8.cloned.1.call-start = ((), (), s32[]{:S(2)}) async-start(), calls=%async_computation.2 | async-start | bytes 4259840 | tf_op jit(solution)/shard_map/all_gather | solution.py:18
  7.3 13.7 %collective-permute-start.1 = (bf16[2,1024]{1,0:T(2,128)(2,1)S(1)}, bf16[2,1024]{1,0:T(2,128)(2,1)S(1)}, u32[]{:S(2)}, u32[]{:S(2)}) collective-permute-start(bf16[2,1024]{1,0:T(2,128)(2,1)S(1)} %slice.146), channel_id=1, source_target_pairs={{0,8},{8,16},{16,24},{24,32},{32,40},{40,48},{48,56},{56,64},{64,7... | collective-permute-start | bytes 12296 | tf_op jit(solution)/shard_map/ppermute | solution.py:13
  11.8 10.2 %collective-permute-start.2 = (bf16[2,1024]{1,0:T(2,128)(2,1)S(1)}, bf16[2,1024]{1,0:T(2,128)(2,1)S(1)}, u32[]{:S(2)}, u32[]{:S(2)}) collective-permute-start(bf16[2,1024]{1,0:T(2,128)(2,1)S(1)} %slice.153), channel_id=1, source_target_pairs={{0,8},{8,16},{16,24},{24,32},{32,40},{40,48},{48,56},{56,64},{64,7... | collective-permute-start | bytes 12296 | tf_op jit(solution)/shard_map/ppermute | solution.py:13
  19.2 293.7 %all-gather.10.cloned.1.call-start = ((), (), s32[]{:S(2)}) async-start(), calls=%async_computation.3 | async-start | bytes 4259840 | tf_op jit(solution)/shard_map/all_gather | solution.py:18
  32.1 36.4 %copy-start.3 = (bf16[128,1024]{1,0:T(8,128)(2,1)S(1)}, bf16[128,1024]{1,0:T(8,128)(2,1)}, u32[]{:S(2)}) copy-start(bf16[128,1024]{1,0:T(8,128)(2,1)} %param.12) | copy-start | bytes 786436
  37.3 38.8 %copy-start.2 = (f32[1024,16]{0,1:T(8,128)S(1)}, f32[1024,16]{0,1:T(8,128)}, u32[]{:S(2)}) copy-start(f32[1024,16]{0,1:T(8,128)} %param.17) | copy-start | bytes 196612
  67.8 0.6 copy-start
  67.8 8.2 %copy-start.1 = (f32[16,1024,16]{1,2,0:T(8,128)S(1)}, f32[16,1024,16]{1,2,0:T(8,128)}, u32[]{:S(2)}) copy-start(f32[16,1024,16]{1,2,0:T(8,128)} %get-tuple-element.132) | copy-start | bytes 3145732
  68.5 398.9 %all-gather.6.cloned.1.call-start = ((), (), s32[]{:S(2)}) async-start(), calls=%async_computation.1 | async-start | bytes 8519680 | tf_op jit(solution)/shard_map/all_gather | solution.py:142
  68.5 22.1 %collective-permute-start = (bf16[2,1024]{1,0:T(2,128)(2,1)S(1)}, bf16[2,1024]{1,0:T(2,128)(2,1)S(1)}, u32[]{:S(2)}, u32[]{:S(2)}) collective-permute-start(bf16[2,1024]{1,0:T(2,128)(2,1)S(1)} %slice.138), channel_id=1, source_target_pairs={{0,8},{8,16},{16,24},{24,32},{32,40},{40,48},{48,56},{56,64},{64,7... | collective-permute-start | bytes 12296 | tf_op jit(solution)/shard_map/ppermute | solution.py:13
Sparse Core Ops, SparseCore 0:
  19.3 149.2 all-gather.7
  171.6 141.2 all-gather.9
  315.9 151.4 all-gather.5
